TPU v7x, 512 devices: a whole 4x8x8 slice. The times are simulated.
512 devices in a mesh: axial: 128 (over z_lo, y, x, core), batch: 4 (over z_hi).
Axes of the slice: x: 4, y: 8, z: 8 (z_hi: 4, z_lo: 2; z = z_hi * 2 + z_lo), core: 2. Of those that a mesh axis runs over, the one named last changes fastest.
Arguments:
- pair: bfloat16 [1024, 256, 128], P(('batch', 'axial')), parts along dimension 0, may hold values from -6 to 6
- residue_mask: int32 [1024], P(('batch', 'axial')), parts along dimension 0, may hold values 0 or 1
- gate_left: bfloat16 [128, 128], replicated, may hold values from -0.5 to 0.5
- proj_left: bfloat16 [128, 128], replicated, may hold values from -0.5 to 0.5
- gate_right: bfloat16 [128, 128], replicated, may hold values from -0.5 to 0.5
- proj_right: bfloat16 [128, 128], replicated, may hold values from -0.5 to 0.5
- gate_out: bfloat16 [128, 128], replicated, may hold values from -0.5 to 0.5
- proj_out: bfloat16 [128, 128], replicated, may hold values from -0.5 to 0.5
Outputs:
- updated: bfloat16 [1024, 256, 128], P('batch', 'axial'), parts along dimension 0
There are 4 independent parts, one for each index of `batch`. A program takes and returns all parts, laid end to end along the dimension named above; an argument that names none is the same for every part. Nothing has to cross between parts.
All inputs are finite; a program needn't handle non-finite values. No bound on the sum of `residue_mask` on one device may be relied on, other than what follows from the above.
Results may differ from a plain program's by a relative error of at most 0.004.
Values may be sent and summed in bfloat16 or wider, within the bound.
A program may use at most 64 MiB of HBM per device.

v0:
```python
import jax
import jax.numpy as jnp
from jax import lax
from jax.sharding import PartitionSpec as P


def layer_norm(values, axis):
    mean = jnp.mean(values, axis=axis, keepdims=True)
    centered = values - mean
    var = jnp.mean(centered * centered, axis=axis, keepdims=True)
    return centered / jnp.sqrt(var + 1e-05)


def body(pair, residue_mask, gate_left, proj_left, gate_right, proj_right, gate_out, proj_out):
    rows = pair.shape[0]
    mask_all = lax.all_gather(residue_mask, "axial", axis=0, tiled=True).astype(jnp.float32)
    first = lax.axis_index("axial") * rows
    mask_rows = lax.dynamic_slice_in_dim(mask_all, first, rows, 0)
    normed = layer_norm(pair.astype(jnp.float32), 2).astype(jnp.bfloat16)
    pair_mask = mask_rows[:, None] * mask_all[None, :]

    def factor(gate_w, proj_w):
        gating = jnp.einsum("rkc,ch->hrk", normed, gate_w, preferred_element_type=jnp.float32)
        values = jnp.einsum("rkc,ch->hrk", normed, proj_w, preferred_element_type=jnp.float32)
        return (jax.nn.sigmoid(gating) * values * pair_mask[None]).astype(jnp.bfloat16)

    left = factor(gate_left, proj_left)
    right = factor(gate_right, proj_right)
    left_all, right_all = (
        lax.all_to_all(left, "axial", split_axis=0, concat_axis=1, tiled=True),
        lax.all_to_all(right, "axial", split_axis=0, concat_axis=1, tiled=True),
    )
    products = jnp.einsum(
        "hik,hjk->hij", left_all, right_all, preferred_element_type=jnp.float32
    ).astype(jnp.bfloat16)
    received = lax.all_to_all(products, "axial", split_axis=1, concat_axis=0, tiled=True)
    prod_normed = layer_norm(received.astype(jnp.float32), 0).astype(jnp.bfloat16)
    update = jnp.einsum("hij,hc->ijc", prod_normed, proj_out, preferred_element_type=jnp.float32)
    gating = jax.nn.sigmoid(
        jnp.einsum("ijc,cd->ijd", normed, gate_out, preferred_element_type=jnp.float32)
    )
    finished = (pair.astype(jnp.float32) + gating * update).astype(jnp.bfloat16)
    return lax.all_to_all(finished, "axial", split_axis=1, concat_axis=0, tiled=True)


def solution(mesh):
    return jax.shard_map(
        body,
        mesh=mesh,
        in_specs=(
            P(("batch", "axial"), None, None),
            P(("batch", "axial")),
            P(),
            P(),
            P(),
            P(),
            P(),
            P(),
        ),
        out_specs=P("batch", "axial", None),
        check_vma=False,
    )
```

profile of v0, /device:TPU:1, one launch (start us, length us, event | category | flops | bytes accessed | tf_op | source)
XLA Modules:
  0.0 112.5 jit_solution(7738016790595958168)
XLA Ops:
  0.0 1.3 %dynamic-slice = u32[1]{0:T(128)} dynamic-slice(u32[512]{0:T(512)} %constant.31, u32[]{:T(128)S(6)} %add.45), dynamic_slice_sizes={1} | dynamic-slice | bytes 12
  2.0 0.9 dynamic-update-slice
  2.8 21.7 %all-reduce = s32[256]{0:T(256)S(1)} all-reduce(s32[256]{0:T(256)S(1)} %dynamic-update-slice), channel_id=1, replica_groups=mesh['axial'=128,'batch'=4] {'axial'}, use_global_device_ids=true, to_apply=%add | all-reduce | flops 256 | bytes 2048
  24.7 1.0 convert_reduce_fusion
  25.8 0.2 fusion.20
  26.0 0.3 fusion.8
  26.4 0.4 copy-done.2
  26.8 0.3 fusion.16
  27.1 0.8 copy.15
  27.9 12.0 %all-to-all-start = ((bf16[128,2,256]{2,1,0:T(2,128)(2,1)}), bf16[128,2,256]{2,1,0:T(2,128)(2,1)S(1)}, u32[]{:S(2)}, u32[]{:S(2)}) async-start(bf16[128,2,256]{2,1,0:T(2,128)(2,1)} %copy.15), calls=%async_computation | async-start | bytes 262144 | tf_op jit(solution)/shard_map/all_to_all | solution.py:30
  39.9 0.3 fusion.5
  40.3 0.4 copy-done.4
  40.7 0.3 fusion.15
  41.0 0.8 copy.16
  41.8 10.6 %all-to-all-done = bf16[128,2,256]{2,1,0:T(2,128)(2,1)S(1)} async-done(((bf16[128,2,256]{2,1,0:T(2,128)(2,1)}), bf16[128,2,256]{2,1,0:T(2,128)(2,1)S(1)}, u32[]{:S(2)}, u32[]{:S(2)}) %all-to-all-start) | async-done | bytes 131104 | tf_op jit(solution)/shard_map/all_to_all | solution.py:30
  52.3 5.6 %all-to-all-start.1 = ((bf16[128,2,256]{2,1,0:T(2,128)(2,1)}), bf16[128,2,256]{2,1,0:T(2,128)(2,1)S(1)}, u32[]{:S(2)}, u32[]{:S(2)}) async-start(bf16[128,2,256]{2,1,0:T(2,128)(2,1)} %copy.16), calls=%async_computation.1 | async-start | bytes 262144 | tf_op jit(solution)/shard_map/all_to_all | solution.py:31
  58.0 12.5 %all-to-all-done.1 = bf16[128,2,256]{2,1,0:T(2,128)(2,1)S(1)} async-done(((bf16[128,2,256]{2,1,0:T(2,128)(2,1)}), bf16[128,2,256]{2,1,0:T(2,128)(2,1)S(1)}, u32[]{:S(2)}, u32[]{:S(2)}) %all-to-all-start.1) | async-done | bytes 131104 | tf_op jit(solution)/shard_map/all_to_all | solution.py:31
  70.5 0.2 fusion.17
  70.7 0.2 copy.23
  70.9 0.5 broadcast.88
  71.5 1.4 %reduce.2 = bf16[256,256]{1,0:T(8,128)(2,1)S(1)} reduce(bf16[256,1,256]{2,1,0:T(2,128)(2,1)S(1)} %bitcast.36, bf16[]{:T(256)} %broadcast.88), dimensions={1}, to_apply=%bitcast.35.reduce_sub_computation | reduce | bytes 262146
  72.9 0.7 reshape.90
  73.6 5.7 %all-to-all-start.2 = ((bf16[128,2,256]{2,1,0:T(2,128)(2,1)}), bf16[128,2,256]{2,1,0:T(2,128)(2,1)S(1)}, u32[]{:S(2)}, u32[]{:S(2)}) async-start(bf16[128,2,256]{2,1,0:T(2,128)(2,1)} %reshape.90), calls=%async_computation.2 | async-start | bytes 262144 | tf_op jit(solution)/shard_map/all_to_all | solution.py:36
  79.3 0.3 fusion.11
  79.6 12.2 %all-to-all-done.2 = bf16[128,2,256]{2,1,0:T(2,128)(2,1)S(1)} async-done(((bf16[128,2,256]{2,1,0:T(2,128)(2,1)}), bf16[128,2,256]{2,1,0:T(2,128)(2,1)S(1)}, u32[]{:S(2)}, u32[]{:S(2)}) %all-to-all-start.2) | async-done | bytes 131104 | tf_op jit(solution)/shard_map/all_to_all | solution.py:36
  91.9 0.7 convert_reduce_fusion.1
  93.0 0.1 reduce_sum.38
  93.1 0.2 multiply_reduce_fusion
  93.4 0.5 copy-done.6
  93.9 0.3 fusion.14
  94.3 17.4 %all_to_all.45 = bf16[2,256,128]{2,0,1:T(2,128)(2,1)S(1)} all-to-all(bf16[2,256,128]{2,0,1:T(2,128)(2,1)S(1)} %copy.19), channel_id=1, replica_groups=mesh['axial'=128,'batch'=4] {'axial'}, dimensions={1} | all-to-all | bytes 262144 | tf_op jit(solution)/shard_map/all_to_all | solution.py:43
  111.8 0.7 copy.20
  (25 shorter events, 0.9 us)
Async XLA Ops:
  0.0 26.0 %copy-start = (bf16[128,128]{1,0:T(8,128)(2,1)S(1)}, bf16[128,128]{1,0:T(8,128)(2,1)}, u32[]{:S(2)}) copy-start(bf16[128,128]{1,0:T(8,128)(2,1)} %param.10) | copy-start | bytes 98308
  0.0 25.8 %copy-start.1 = (bf16[2,256,128]{2,1,0:T(8,128)(2,1)S(1)}, bf16[2,256,128]{2,1,0:T(8,128)(2,1)}, u32[]{:S(2)}) copy-start(bf16[2,256,128]{2,1,0:T(8,128)(2,1)} %param.8) | copy-start | bytes 393220
  26.0 0.8 copy-start.2
  27.9 12.0 %copy-start.3 = (bf16[128,128]{1,0:T(8,128)(2,1)S(1)}, bf16[128,128]{1,0:T(8,128)(2,1)}, u32[]{:S(2)}) copy-start(bf16[128,128]{1,0:T(8,128)(2,1)} %param.12) | copy-start | bytes 98308
  27.9 24.4 %all-to-all-start = ((bf16[128,2,256]{2,1,0:T(2,128)(2,1)}), bf16[128,2,256]{2,1,0:T(2,128)(2,1)S(1)}, u32[]{:S(2)}, u32[]{:S(2)}) async-start(bf16[128,2,256]{2,1,0:T(2,128)(2,1)} %copy.15), calls=%async_computation | async-start | bytes 262144 | tf_op jit(solution)/shard_map/all_to_all | solution.py:30
  39.9 0.8 copy-start.4
  52.3 18.1 %all-to-all-start.1 = ((bf16[128,2,256]{2,1,0:T(2,128)(2,1)}), bf16[128,2,256]{2,1,0:T(2,128)(2,1)S(1)}, u32[]{:S(2)}, u32[]{:S(2)}) async-start(bf16[128,2,256]{2,1,0:T(2,128)(2,1)} %copy.16), calls=%async_computation.1 | async-start | bytes 262144 | tf_op jit(solution)/shard_map/all_to_all | solution.py:31
  73.6 5.7 %copy-start.5 = (bf16[128,128]{1,0:T(8,128)(2,1)S(1)}, bf16[128,128]{1,0:T(8,128)(2,1)}, u32[]{:S(2)}) copy-start(bf16[128,128]{1,0:T(8,128)(2,1)} %param.14) | copy-start | bytes 98308
  73.6 18.2 %all-to-all-start.2 = ((bf16[128,2,256]{2,1,0:T(2,128)(2,1)}), bf16[128,2,256]{2,1,0:T(2,128)(2,1)S(1)}, u32[]{:S(2)}, u32[]{:S(2)}) async-start(bf16[128,2,256]{2,1,0:T(2,128)(2,1)} %reshape.90), calls=%async_computation.2 | async-start | bytes 262144 | tf_op jit(solution)/shard_map/all_to_all | solution.py:36
  93.1 0.8 copy-start.6
where the time goes:
time: 113 us
  blocking collectives  39.2 us (35%)
  waiting for transfers between devices  35.2 us (31%)
  starting transfers between devices  23.2 us (21%)
  local copies, waits for them, and re-layouts  7.93 us (7%)
  other arithmetic  3.92 us (3%)
  matrix products  2.17 us (2%)
    unnamed x1, blocking collectives  21.7 us
    all_to_all x1, blocking collectives, body(): lax.all_to_all(finished, 'axial', split_axis=1, concat_axis=0, tiled=True)  17.4 us
    all_to_all x1, waiting for transfers between devices, body(): lax.all_to_all(right, 'axial', split_axis=0, concat_axis=1, tiled=True)  12.5 us
    all_to_all x1, waiting for transfers between devices, body(): lax.all_to_all(products, 'axial', split_axis=1, concat_axis=0, tiled=True)  12.2 us
    all_to_all x1, starting transfers between devices, body(): lax.all_to_all(left, 'axial', split_axis=0, concat_axis=1, tiled=True)  12 us
    all_to_all x1, waiting for transfers between devices, body(): lax.all_to_all(left, 'axial', split_axis=0, concat_axis=1, tiled=True)  10.6 us
    all_to_all x1, starting transfers between devices, body(): lax.all_to_all(products, 'axial', split_axis=1, concat_axis=0, tiled=True)  5.69 us
    all_to_all x1, starting transfers between devices, body(): lax.all_to_all(right, 'axial', split_axis=0, concat_axis=1, tiled=True)  5.56 us
  transfers between devices with their start and end apart: 3, of which 3 were waited for; matrix products, arithmetic and copies ran while one was open for 2% of the time, Pallas kernels for 0%

commit v1 on v0

v1 whole, which is shorter than its diff:
```python
import itertools

import jax
import jax.numpy as jnp
from jax import lax
from jax.experimental import pallas as pl
from jax.experimental.pallas import tpu as pltpu
from jax.sharding import PartitionSpec as P

MESH = pl.DeviceIdType.MESH
F32, BF16 = jnp.float32, jnp.bfloat16
NZ, NY, NX, NC = 2, 8, 4, 2
D = NZ * NY * NX * NC
CH = 128
Y_ORDER = (4, 3, 5, 2, 6, 1, 7, 0)
X_ORDER = (2, 1, 3, 0)
PEERS = tuple(
    (dz, dy, dx, dc)
    for dy, dx, dz, dc in itertools.product(Y_ORDER, X_ORDER, (1, 0), (0, 1))
    if dz + dy + dx + dc
)
NT = (((1,), (1,)), ((), ()))
TN = (((0,), (0,)), ((), ()))


def layer_norm(values, axis):
    mean = jnp.mean(values, axis=axis, keepdims=True)
    centered = values - mean
    var = jnp.mean(centered * centered, axis=axis, keepdims=True)
    return centered * lax.rsqrt(var + 1e-05)


def kernel(
    pair_hbm, mask_ref, gl_hbm, pl_hbm, gr_hbm, pr_hbm, go_hbm, po_hbm, out_ref,
    pair_v, w_v, msg, fac, prod, prods, pairs, mx, my, mz, mask_v, s8, s4, gate_v,
    load_sem, wload_sem, send_sem, fac_sem, prods_sem, pairs_sem, mask_sem,
):
    me = lax.axis_index("axial")
    z, y = lax.div(me, 64), lax.rem(lax.div(me, 8), 8)
    x, c = lax.rem(lax.div(me, 2), 4), lax.rem(me, 2)
    zt = [64 * lax.rem(z + k, 2) for k in range(NZ)]
    yt = [8 * lax.rem(y + k, 8) for k in range(NY)]
    xt = [2 * lax.rem(x + k, 4) for k in range(NX)]
    ct = [lax.rem(c + k, 2) for k in range(NC)]
    targets = [zt[dz] + yt[dy] + xt[dx] + ct[dc] for dz, dy, dx, dc in PEERS]

    load = pltpu.make_async_copy(pair_hbm, pair_v, load_sem)
    load.start()
    wloads = [
        pltpu.make_async_copy(ref, w_v.at[i], wload_sem.at[i])
        for i, ref in enumerate((gl_hbm, pl_hbm, gr_hbm, pr_hbm, go_hbm, po_hbm))
    ]
    for w in wloads:
        w.start()
    barrier = pltpu.get_barrier_semaphore()
    for t in targets:
        pl.semaphore_signal(barrier, inc=1, device_id={"axial": t}, device_id_type=MESH)

    def send(src, dst, sem, recv_sem, t):
        pltpu.make_async_remote_copy(
            src_ref=src, dst_ref=dst, send_sem=sem, recv_sem=recv_sem,
            device_id={"axial": t}, device_id_type=MESH,
        ).start()

    def landed(ref, sem):
        pltpu.make_async_copy(ref, ref, sem).wait()

    load.wait()
    normed = layer_norm(pair_v.reshape(512, 128)[...].astype(F32), 1).astype(BF16)
    for w in wloads:
        w.wait()
    for f in range(2):
        gating = lax.dot_general(
            w_v[2 * f], normed, (((0,), (1,)), ((), ())), preferred_element_type=F32
        )
        values = lax.dot_general(
            w_v[2 * f + 1], normed, (((0,), (1,)), ((), ())), preferred_element_type=F32
        )
        factor = jax.nn.sigmoid(gating) * values
        for r in range(2):
            row_mask = mask_ref[r].astype(F32)
            for kh in range(2):
                q = 2 * r + kh
                s8[pl.ds(4 * f + q, 128, stride=8), :] = (
                    factor[:, 128 * q : 128 * q + 128] * row_mask
                )
    msg.reshape(1024, 128)[...] = s8[...].astype(BF16)

    k_index = lax.broadcasted_iota(jnp.int32, (2, 128), 0) * 128 + lax.broadcasted_iota(
        jnp.int32, (2, 128), 1
    )
    own_mask = jnp.where(k_index == 2 * me, mask_ref[0], 0) + jnp.where(
        k_index == 2 * me + 1, mask_ref[1], 0
    )
    xc = 2 * x + c
    mx[xc] = own_mask.astype(F32)

    pl.semaphore_wait(barrier, D - 1)

    for dx, dc in itertools.product(range(NX), range(NC)):
        if dx + dc:
            send(mx.at[xc], mx.at[xc], mask_sem.at[0], mask_sem.at[1], zt[0] + yt[0] + xt[dx] + ct[dc])
    for t in targets:
        send(msg.at[t], fac.at[me], send_sem.at[0], fac_sem, t)
    pltpu.make_async_copy(msg.at[me], fac.at[me], fac_sem).start()

    landed(mx.at[pl.ds(0, 7)], mask_sem.at[1])
    my[y] = jnp.sum(mx[...], axis=0)
    for dy in range(1, NY):
        send(my.at[y], my.at[y], mask_sem.at[2], mask_sem.at[3], zt[0] + yt[dy] + xt[0] + ct[0])
    for t in targets:
        send(pair_v.at[:, t], pairs.at[me], send_sem.at[1], pairs_sem, t)
    pltpu.make_async_copy(pair_v.at[:, me], pairs.at[me], pairs_sem).start()
    landed(my.at[pl.ds(0, 7)], mask_sem.at[3])
    mz[z] = jnp.sum(my[...], axis=0)
    send(mz.at[z], mz.at[z], mask_sem.at[4], mask_sem.at[5], zt[1] + yt[0] + xt[0] + ct[0])
    landed(mz.at[pl.ds(0, 1)], mask_sem.at[5])
    mask_v[...] = jnp.sum(mz[...], axis=0)

    landed(fac, fac_sem)
    s8[...] = fac.reshape(1024, 128)[...].astype(F32)
    halves = [s8[pl.ds(q, 128, stride=8), :] for q in range(8)]
    lefts = [
        jnp.concatenate(
            [halves[2 * r + kh] * mask_v[kh : kh + 1, :] for kh in range(2)], axis=1
        )
        for r in range(2)
    ]
    left = jnp.concatenate(lefts, axis=0).astype(BF16)
    rights = [jnp.concatenate(halves[4 + 2 * r : 6 + 2 * r], axis=1) for r in range(2)]
    right = jnp.concatenate(rights, axis=0).astype(BF16)
    product = lax.dot_general(right, left, NT, preferred_element_type=F32)
    for rj, ri in itertools.product(range(2), range(2)):
        s4[pl.ds(2 * rj + ri, 128, stride=4), :] = product[
            128 * rj : 128 * rj + 128, 128 * ri : 128 * ri + 128
        ]
    prod.reshape(512, 128)[...] = s4[...].astype(BF16)
    for t in targets:
        send(prod.at[t], prods.at[me], send_sem.at[2], prods_sem, t)
    pltpu.make_async_copy(prod.at[me], prods.at[me], prods_sem).start()

    landed(pairs, pairs_sem)
    columns = pairs.reshape(512, 128)
    normed = layer_norm(columns[...].astype(F32), 1).astype(BF16)
    gate_v[...] = jax.nn.sigmoid(
        jnp.dot(normed, w_v[4], preferred_element_type=F32)
    )

    landed(prods, prods_sem)
    s4[...] = prods.reshape(512, 128)[...].astype(F32)
    update = []
    for rj, ri in itertools.product(range(2), range(2)):
        channels = s4[pl.ds(2 * rj + ri, 128, stride=4), :]
        update.append(
            lax.dot_general(
                layer_norm(channels, 0).astype(BF16), w_v[5], TN, preferred_element_type=F32
            )
        )
    for (rj, ri), part in zip(itertools.product(range(2), range(2)), update):
        s4[pl.ds(2 * ri + rj, 128, stride=4), :] = part
    out_ref[...] = (columns[...].astype(F32) + gate_v[...] * s4[...]).astype(BF16)

    landed(msg.at[pl.ds(0, D - 1)], send_sem.at[0])
    landed(pairs.at[pl.ds(0, D - 1)], send_sem.at[1])
    landed(prod.at[pl.ds(0, D - 1)], send_sem.at[2])
    landed(mx.at[pl.ds(0, 7)], mask_sem.at[0])
    landed(my.at[pl.ds(0, 7)], mask_sem.at[2])
    landed(mz.at[pl.ds(0, 1)], mask_sem.at[4])


def body(pair, residue_mask, *weights):
    hbm = pl.BlockSpec(memory_space=pltpu.HBM)
    out = pl.pallas_call(
        kernel,
        out_shape=jax.ShapeDtypeStruct((512, 128), BF16),
        in_specs=[hbm, pl.BlockSpec(memory_space=pltpu.SMEM)] + [hbm] * 6,
        out_specs=pl.BlockSpec(memory_space=pltpu.VMEM),
        scratch_shapes=[
            pltpu.VMEM((2, D, 2, 128), BF16),
            pltpu.VMEM((6, 128, 128), BF16),
            pltpu.VMEM((D, 8, 128), BF16),
            pltpu.VMEM((D, 8, 128), BF16),
            pltpu.VMEM((D, 4, 128), BF16),
            pltpu.VMEM((D, 4, 128), BF16),
            pltpu.VMEM((D, 2, 2, 128), BF16),
            pltpu.VMEM((8, 2, 128), F32),
            pltpu.VMEM((8, 2, 128), F32),
            pltpu.VMEM((2, 2, 128), F32),
            pltpu.VMEM((2, 128), F32),
            pltpu.VMEM((1024, 128), F32),
            pltpu.VMEM((512, 128), F32),
            pltpu.VMEM((512, 128), F32),
            pltpu.SemaphoreType.DMA,
            pltpu.SemaphoreType.DMA((6,)),
            pltpu.SemaphoreType.DMA((3,)),
            pltpu.SemaphoreType.DMA,
            pltpu.SemaphoreType.DMA,
            pltpu.SemaphoreType.DMA,
            pltpu.SemaphoreType.DMA((6,)),
        ],
        compiler_params=pltpu.CompilerParams(
            collective_id=0, has_side_effects=True, vmem_limit_bytes=60 << 20
        ),
    )(pair.reshape(2, D, 2, 128), residue_mask, *weights)
    return out.reshape(256, 2, 128)


def solution(mesh):
    return jax.shard_map(
        body,
        mesh=mesh,
        in_specs=(P(("batch", "axial"), None, None), P(("batch", "axial")))
        + (P(),) * 6,
        out_specs=P("batch", "axial", None),
        check_vma=False,
    )
```

time: 113 us -> 35 us (0.31)
  blocking collectives: 39.2 us -> 0 us
  waiting for transfers between devices: 35.2 us -> 0 us
  Pallas kernels: 0 us -> 33.2 us
  starting transfers between devices: 23.2 us -> 0 us
  local copies, waits for them, and re-layouts: 7.93 us -> 1.65 us
  other arithmetic: 3.92 us -> 0 us
  matrix products: 2.17 us -> 0 us
    all_to_all x3 -> x0, waiting for transfers between devices: 35.2 us -> none  [the longest x1 12.5 us: body(): lax.all_to_all(right, 'axial', split_axis=0, concat_axis=1, tiled=True)]
    pallas_call x0 -> x1, Pallas kernels: none -> 33.2 us  [body(): pl.pallas_call(kernel, out_shape=jax.ShapeDtypeStruct((512, 128), BF16),...]
    all_to_all x3 -> x0, starting transfers between devices: 23.2 us -> none  [the longest x1 12 us: body(): lax.all_to_all(left, 'axial', split_axis=0, concat_axis=1, tiled=True)]
    unnamed x1 -> x0, blocking collectives: 21.7 us -> none
    all_to_all x1 -> x0, blocking collectives: 17.4 us -> none  [body(): lax.all_to_all(finished, 'axial', split_axis=1, concat_axis=0, tiled=True)]
    unnamed x20 -> x1, local copies, waits for them, and re-layouts: 4.81 us -> 1.65 us
    convert_element_type x6 -> x0, local copies, waits for them, and re-layouts: 2.18 us -> none  [the longest x2 1.56 us: factor(): (jax.nn.sigmoid(gating) * values * pair_mask[None]).astype(jnp.bfloat16)]
    dot_general x7 -> x0, matrix products: 2.17 us -> none  [the longest x2 0.67 us: factor(): jnp.einsum('rkc,ch->hrk', normed, gate_w, preferred_element_type=jnp.floa...]
  transfers between devices with their start and end apart: 3 -> 0, of which waited for: 3 -> 0; matrix products, arithmetic and copies ran while one was open for 2% -> 0% of each run, Pallas kernels for 0% -> 0%
where the time goes in v1:
time: 35 us; the launch traced here: 34.8 us
  Pallas kernels  33.2 us (95%)
  local copies, waits for them, and re-layouts  1.65 us (5%)
    pallas_call x1, Pallas kernels, body(): pl.pallas_call(kernel, out_shape=jax.ShapeDtypeStruct((512, 128), BF16),...  33.2 us
    unnamed x1, local copies, waits for them, and re-layouts  1.65 us

profile of v1, /device:TPU:1, one launch (start us, length us, event | category | flops | bytes accessed | tf_op | source)
XLA Modules:
  0.0 34.8 jit_solution(8014481688427575784)
XLA Ops:
  0.0 33.2 %shard_map.82 = bf16[512,128]{1,0:T(8,128)(2,1)} custom-call(bf16[2,128,2,128]{3,2,1,0:T(2,128)(2,1)} %bitcast.3, s32[2]{0:T(128)} %mask_ref.1, bf16[128,128]{1,0:T(8,128)(2,1)} %gl_hbm.1, bf16[128,128]{1,0:T(8,128)(2,1)} %pl_hbm.1, bf16[128,128]{1,0:T(8,128)(2,1)} %gr_hbm.1, bf16[128,128]{1,0:T(8,128)(2,1)} %pr_hbm.1, bf16[128,128]{1,0:T(8,128)(2,1)} %go_hbm.1, ...), custom_call_target="tpu_custom_call" | custom-call | tf_op jit(solution)/shard_map/pallas_call | solution.py:173
  33.2 1.7 %copy.10 = bf16[256,2,128]{2,1,0:T(2,128)(2,1)} copy(bf16[256,2,128]{2,1,0:T(2,128)(2,1)} %bitcast.2) | data formatting | bytes 262144

commit v2 on v1

--- a/solution.py
+++ b/solution.py
@@ -19,6 +19,7 @@
     for dy, dx, dz, dc in itertools.product(Y_ORDER, X_ORDER, (1, 0), (0, 1))
     if dz + dy + dx + dc
 )
+EARLY = 112
 NT = (((1,), (1,)), ((), ()))
 TN = (((0,), (0,)), ((), ()))
 
@@ -32,7 +33,7 @@
 
 def kernel(
     pair_hbm, mask_ref, gl_hbm, pl_hbm, gr_hbm, pr_hbm, go_hbm, po_hbm, out_ref,
-    pair_v, w_v, msg, fac, prod, prods, pairs, mx, my, mz, mask_v, s8, s4, gate_v,
+    pair_v, w_v, msg, fac, prod, prods, pairs, mx, my, mask_v, s8, s4, gate_v,
     load_sem, wload_sem, send_sem, fac_sem, prods_sem, pairs_sem, mask_sem,
 ):
     me = lax.axis_index("axial")
@@ -44,6 +45,10 @@
     ct = [lax.rem(c + k, 2) for k in range(NC)]
     targets = [zt[dz] + yt[dy] + xt[dx] + ct[dc] for dz, dy, dx, dc in PEERS]
 
+    barrier = pltpu.get_barrier_semaphore()
+    for t in targets:
+        pl.semaphore_signal(barrier, inc=1, device_id={"axial": t}, device_id_type=MESH)
+
     load = pltpu.make_async_copy(pair_hbm, pair_v, load_sem)
     load.start()
     wloads = [
@@ -52,9 +57,6 @@
     ]
     for w in wloads:
         w.start()
-    barrier = pltpu.get_barrier_semaphore()
-    for t in targets:
-        pl.semaphore_signal(barrier, inc=1, device_id={"axial": t}, device_id_type=MESH)
 
     def send(src, dst, sem, recv_sem, t):
         pltpu.make_async_remote_copy(
@@ -92,30 +94,31 @@
     own_mask = jnp.where(k_index == 2 * me, mask_ref[0], 0) + jnp.where(
         k_index == 2 * me + 1, mask_ref[1], 0
     )
-    xc = 2 * x + c
+    xc, zy = 2 * x + c, 8 * z + y
     mx[xc] = own_mask.astype(F32)
 
     pl.semaphore_wait(barrier, D - 1)
 
     for dx, dc in itertools.product(range(NX), range(NC)):
         if dx + dc:
-            send(mx.at[xc], mx.at[xc], mask_sem.at[0], mask_sem.at[1], zt[0] + yt[0] + xt[dx] + ct[dc])
-    for t in targets:
+            t = zt[0] + yt[0] + xt[dx] + ct[dc]
+            send(mx.at[xc], mx.at[xc], mask_sem.at[0], mask_sem.at[1], t)
+    for t in targets[:EARLY]:
+        send(msg.at[t], fac.at[me], send_sem.at[0], fac_sem, t)
+    landed(mx.at[pl.ds(0, 7)], mask_sem.at[1])
+    my[zy] = jnp.sum(mx[...], axis=0)
+    for dy, dz in itertools.product(Y_ORDER, (1, 0)):
+        if dy + dz:
+            t = zt[dz] + yt[dy] + xt[0] + ct[0]
+            send(my.at[zy], my.at[zy], mask_sem.at[2], mask_sem.at[3], t)
+    for t in targets[EARLY:]:
         send(msg.at[t], fac.at[me], send_sem.at[0], fac_sem, t)
     pltpu.make_async_copy(msg.at[me], fac.at[me], fac_sem).start()
-
-    landed(mx.at[pl.ds(0, 7)], mask_sem.at[1])
-    my[y] = jnp.sum(mx[...], axis=0)
-    for dy in range(1, NY):
-        send(my.at[y], my.at[y], mask_sem.at[2], mask_sem.at[3], zt[0] + yt[dy] + xt[0] + ct[0])
     for t in targets:
         send(pair_v.at[:, t], pairs.at[me], send_sem.at[1], pairs_sem, t)
     pltpu.make_async_copy(pair_v.at[:, me], pairs.at[me], pairs_sem).start()
-    landed(my.at[pl.ds(0, 7)], mask_sem.at[3])
-    mz[z] = jnp.sum(my[...], axis=0)
-    send(mz.at[z], mz.at[z], mask_sem.at[4], mask_sem.at[5], zt[1] + yt[0] + xt[0] + ct[0])
-    landed(mz.at[pl.ds(0, 1)], mask_sem.at[5])
-    mask_v[...] = jnp.sum(mz[...], axis=0)
+    landed(my.at[pl.ds(0, 15)], mask_sem.at[3])
+    mask_v[...] = jnp.sum(my[...], axis=0)
 
     landed(fac, fac_sem)
     s8[...] = fac.reshape(1024, 128)[...].astype(F32)
@@ -164,15 +167,18 @@
     landed(pairs.at[pl.ds(0, D - 1)], send_sem.at[1])
     landed(prod.at[pl.ds(0, D - 1)], send_sem.at[2])
     landed(mx.at[pl.ds(0, 7)], mask_sem.at[0])
-    landed(my.at[pl.ds(0, 7)], mask_sem.at[2])
-    landed(mz.at[pl.ds(0, 1)], mask_sem.at[4])
+    landed(my.at[pl.ds(0, 15)], mask_sem.at[2])
 
 
 def body(pair, residue_mask, *weights):
     hbm = pl.BlockSpec(memory_space=pltpu.HBM)
+    inputs = [
+        pltpu.with_memory_space_constraint(v, pltpu.HBM)
+        for v in (pair.reshape(2, D, 2, 128), *weights)
+    ]
     out = pl.pallas_call(
         kernel,
-        out_shape=jax.ShapeDtypeStruct((512, 128), BF16),
+        out_shape=pltpu.VMEM((512, 128), BF16),
         in_specs=[hbm, pl.BlockSpec(memory_space=pltpu.SMEM)] + [hbm] * 6,
         out_specs=pl.BlockSpec(memory_space=pltpu.VMEM),
         scratch_shapes=[
@@ -184,8 +190,7 @@
             pltpu.VMEM((D, 4, 128), BF16),
             pltpu.VMEM((D, 2, 2, 128), BF16),
             pltpu.VMEM((8, 2, 128), F32),
-            pltpu.VMEM((8, 2, 128), F32),
-            pltpu.VMEM((2, 2, 128), F32),
+            pltpu.VMEM((16, 2, 128), F32),
             pltpu.VMEM((2, 128), F32),
             pltpu.VMEM((1024, 128), F32),
             pltpu.VMEM((512, 128), F32),
@@ -196,12 +201,12 @@
             pltpu.SemaphoreType.DMA,
             pltpu.SemaphoreType.DMA,
             pltpu.SemaphoreType.DMA,
-            pltpu.SemaphoreType.DMA((6,)),
+            pltpu.SemaphoreType.DMA((4,)),
         ],
         compiler_params=pltpu.CompilerParams(
             collective_id=0, has_side_effects=True, vmem_limit_bytes=60 << 20
         ),
-    )(pair.reshape(2, D, 2, 128), residue_mask, *weights)
+    )(inputs[0], residue_mask, *inputs[1:])
     return out.reshape(256, 2, 128)
 
 

time: 35 us -> 31.2 us (0.89)
  Pallas kernels: 33.2 us -> 30.4 us
  local copies, waits for them, and re-layouts: 1.65 us -> 0.66 us
    pallas_call x1, Pallas kernels: 33.2 us -> 30.4 us  [body(): pl.pallas_call(kernel, out_shape=pltpu.VMEM((512, 128), BF16), in_specs=[...]
    unnamed x1, local copies, waits for them, and re-layouts: 1.65 us -> 0.66 us
where the time goes in v2:
time: 31.2 us; the launch traced here: 31.1 us
  Pallas kernels  30.4 us (97%)
  local copies, waits for them, and re-layouts  0.66 us (2%)
    pallas_call x1, Pallas kernels, body(): pl.pallas_call(kernel, out_shape=pltpu.VMEM((512, 128), BF16), in_specs=[...  30.4 us
    unnamed x1, local copies, waits for them, and re-layouts  0.66 us

profile of v2, /device:TPU:1, one launch (start us, length us, event | category | flops | bytes accessed | tf_op | source)
XLA Modules:
  0.0 31.1 jit_solution(8110840080798680455)
XLA Ops:
  0.0 30.4 %shard_map.82 = bf16[512,128]{1,0:T(8,128)(2,1)S(1)} custom-call(bf16[2,128,2,128]{3,2,1,0:T(2,128)(2,1)} %bitcast.3, s32[2]{0:T(128)} %mask_ref.1, bf16[128,128]{1,0:T(8,128)(2,1)} %gl_hbm.1, bf16[128,128]{1,0:T(8,128)(2,1)} %pl_hbm.1, bf16[128,128]{1,0:T(8,128)(2,1)} %gr_hbm.1, bf16[128,128]{1,0:T(8,128)(2,1)} %pr_hbm.1, bf16[128,128]{1,0:T(8,128)(2,1)} %go_hbm.1, ...), custom_call_target="tpu_custom_call" | custom-call | tf_op jit(solution)/shard_map/pallas_call | solution.py:179
  30.4 0.7 %copy.10 = bf16[256,2,128]{2,1,0:T(2,128)(2,1)} copy(bf16[256,2,128]{2,1,0:T(2,128)(2,1)S(1)} %bitcast.2) | data formatting | bytes 262144

commit v3 on v2

--- a/solution.py
+++ b/solution.py
@@ -32,9 +32,9 @@
 
 
 def kernel(
-    pair_hbm, mask_ref, gl_hbm, pl_hbm, gr_hbm, pr_hbm, go_hbm, po_hbm, out_ref,
-    pair_v, w_v, msg, fac, prod, prods, pairs, mx, my, mask_v, s8, s4, gate_v,
-    load_sem, wload_sem, send_sem, fac_sem, prods_sem, pairs_sem, mask_sem,
+    pair_hbm, mask_hbm, gl_hbm, pl_hbm, gr_hbm, pr_hbm, go_hbm, po_hbm, out_ref,
+    mask_ref, pair_v, w_v, msg, fac, prod, prods, pairs, mx, my, mask_v, s8, s4, gate_v,
+    load_sem, mask_load_sem, wload_sem, send_sem, fac_sem, prods_sem, pairs_sem, mask_sem,
 ):
     me = lax.axis_index("axial")
     z, y = lax.div(me, 64), lax.rem(lax.div(me, 8), 8)
@@ -51,6 +51,8 @@
 
     load = pltpu.make_async_copy(pair_hbm, pair_v, load_sem)
     load.start()
+    mask_load = pltpu.make_async_copy(mask_hbm, mask_ref, mask_load_sem)
+    mask_load.start()
     wloads = [
         pltpu.make_async_copy(ref, w_v.at[i], wload_sem.at[i])
         for i, ref in enumerate((gl_hbm, pl_hbm, gr_hbm, pr_hbm, go_hbm, po_hbm))
@@ -71,6 +73,7 @@
     normed = layer_norm(pair_v.reshape(512, 128)[...].astype(F32), 1).astype(BF16)
     for w in wloads:
         w.wait()
+    mask_load.wait()
     for f in range(2):
         gating = lax.dot_general(
             w_v[2 * f], normed, (((0,), (1,)), ((), ())), preferred_element_type=F32
@@ -138,8 +141,17 @@
             128 * rj : 128 * rj + 128, 128 * ri : 128 * ri + 128
         ]
     prod.reshape(512, 128)[...] = s4[...].astype(BF16)
-    for t in targets:
-        send(prod.at[t], prods.at[me], send_sem.at[2], prods_sem, t)
+    for pz, py in [(0, 0), (0, 1), (0, 2), (0, 3), (1, 0), (0, 7), (1, 1), (0, 6), (0, 5), (0, 4), (1, 2), (1, 3), (1, 7), (1, 6), (1, 5), (1, 4)]:
+        for dx, dc in itertools.product(X_ORDER, (1, 0)):
+            t = 64 * pz + 8 * py + xt[dx] + ct[dc]
+
+            def send_prod(t=t):
+                send(prod.at[t], prods.at[me], send_sem.at[2], prods_sem, t)
+
+            if dx + dc:
+                send_prod()
+            else:
+                pl.when(t != me)(send_prod)
     pltpu.make_async_copy(prod.at[me], prods.at[me], prods_sem).start()
 
     landed(pairs, pairs_sem)
@@ -174,14 +186,15 @@
     hbm = pl.BlockSpec(memory_space=pltpu.HBM)
     inputs = [
         pltpu.with_memory_space_constraint(v, pltpu.HBM)
-        for v in (pair.reshape(2, D, 2, 128), *weights)
+        for v in (pair.reshape(2, D, 2, 128), residue_mask, *weights)
     ]
     out = pl.pallas_call(
         kernel,
         out_shape=pltpu.VMEM((512, 128), BF16),
-        in_specs=[hbm, pl.BlockSpec(memory_space=pltpu.SMEM)] + [hbm] * 6,
+        in_specs=[hbm] * 8,
         out_specs=pl.BlockSpec(memory_space=pltpu.VMEM),
         scratch_shapes=[
+            pltpu.SMEM((2,), jnp.int32),
             pltpu.VMEM((2, D, 2, 128), BF16),
             pltpu.VMEM((6, 128, 128), BF16),
             pltpu.VMEM((D, 8, 128), BF16),
@@ -196,6 +209,7 @@
             pltpu.VMEM((512, 128), F32),
             pltpu.VMEM((512, 128), F32),
             pltpu.SemaphoreType.DMA,
+            pltpu.SemaphoreType.DMA,
             pltpu.SemaphoreType.DMA((6,)),
             pltpu.SemaphoreType.DMA((3,)),
             pltpu.SemaphoreType.DMA,
@@ -206,7 +220,7 @@
         compiler_params=pltpu.CompilerParams(
             collective_id=0, has_side_effects=True, vmem_limit_bytes=60 << 20
         ),
-    )(inputs[0], residue_mask, *inputs[1:])
+    )(*inputs)
     return out.reshape(256, 2, 128)
 
 

time: 31.2 us -> 30.2 us (0.968)
  Pallas kernels: 30.4 us -> 29.5 us
    pallas_call x1, Pallas kernels: 30.4 us -> 29.5 us  [body(): pl.pallas_call(kernel, out_shape=pltpu.VMEM((512, 128), BF16), in_specs=[...]
where the time goes in v3:
time: 30.2 us; the launch traced here: 30.1 us
  Pallas kernels  29.5 us (98%)
  local copies, waits for them, and re-layouts  0.66 us (2%)
    pallas_call x1, Pallas kernels, body(): pl.pallas_call(kernel, out_shape=pltpu.VMEM((512, 128), BF16), in_specs=[...  29.5 us
    unnamed x1, local copies, waits for them, and re-layouts  0.66 us

profile of v3, /device:TPU:1, one launch (start us, length us, event | category | flops | bytes accessed | tf_op | source)
XLA Modules:
  0.0 30.1 jit_solution(16057373518346858041)
XLA Ops:
  0.0 29.5 %shard_map.82 = bf16[512,128]{1,0:T(8,128)(2,1)S(1)} custom-call(bf16[2,128,2,128]{3,2,1,0:T(2,128)(2,1)} %bitcast.3, s32[2]{0:T(128)} %mask_hbm.1, bf16[128,128]{1,0:T(8,128)(2,1)} %gl_hbm.1, bf16[128,128]{1,0:T(8,128)(2,1)} %pl_hbm.1, bf16[128,128]{1,0:T(8,128)(2,1)} %gr_hbm.1, bf16[128,128]{1,0:T(8,128)(2,1)} %pr_hbm.1, bf16[128,128]{1,0:T(8,128)(2,1)} %go_hbm.1, ...), custom_call_target="tpu_custom_call" | custom-call | tf_op jit(solution)/shard_map/pallas_call | solution.py:191
  29.5 0.7 %copy.10 = bf16[256,2,128]{2,1,0:T(2,128)(2,1)} copy(bf16[256,2,128]{2,1,0:T(2,128)(2,1)S(1)} %bitcast.2) | data formatting | bytes 262144

commit v4 on v3

--- a/solution.py
+++ b/solution.py
@@ -19,7 +19,7 @@
     for dy, dx, dz, dc in itertools.product(Y_ORDER, X_ORDER, (1, 0), (0, 1))
     if dz + dy + dx + dc
 )
-EARLY = 112
+EARLY = 60
 NT = (((1,), (1,)), ((), ()))
 TN = (((0,), (0,)), ((), ()))
 

time: 30.2 us -> 29.7 us (0.983)
  Pallas kernels: 29.5 us -> 28.9 us
    pallas_call x1, Pallas kernels: 29.5 us -> 28.9 us  [body(): pl.pallas_call(kernel, out_shape=pltpu.VMEM((512, 128), BF16), in_specs=[...]
where the time goes in v4:
time: 29.7 us; the launch traced here: 29.6 us
  Pallas kernels  28.9 us (97%)
  local copies, waits for them, and re-layouts  0.66 us (2%)
    pallas_call x1, Pallas kernels, body(): pl.pallas_call(kernel, out_shape=pltpu.VMEM((512, 128), BF16), in_specs=[...  28.9 us
    unnamed x1, local copies, waits for them, and re-layouts  0.66 us

profile of v4, /device:TPU:1, one launch (start us, length us, event | category | flops | bytes accessed | tf_op | source)
XLA Modules:
  0.0 29.6 jit_solution(3432545460294298058)
XLA Ops:
  0.0 28.9 %shard_map.82 = bf16[512,128]{1,0:T(8,128)(2,1)S(1)} custom-call(bf16[2,128,2,128]{3,2,1,0:T(2,128)(2,1)} %bitcast.3, s32[2]{0:T(128)} %mask_hbm.1, bf16[128,128]{1,0:T(8,128)(2,1)} %gl_hbm.1, bf16[128,128]{1,0:T(8,128)(2,1)} %pl_hbm.1, bf16[128,128]{1,0:T(8,128)(2,1)} %gr_hbm.1, bf16[128,128]{1,0:T(8,128)(2,1)} %pr_hbm.1, bf16[128,128]{1,0:T(8,128)(2,1)} %go_hbm.1, ...), custom_call_target="tpu_custom_call" | custom-call | tf_op jit(solution)/shard_map/pallas_call | solution.py:191
  28.9 0.7 %copy.10 = bf16[256,2,128]{2,1,0:T(2,128)(2,1)} copy(bf16[256,2,128]{2,1,0:T(2,128)(2,1)S(1)} %bitcast.2) | data formatting | bytes 262144

commit v5 on v4

--- a/solution.py
+++ b/solution.py
@@ -15,9 +15,16 @@
 Y_ORDER = (4, 3, 5, 2, 6, 1, 7, 0)
 X_ORDER = (2, 1, 3, 0)
 PEERS = tuple(
-    (dz, dy, dx, dc)
-    for dy, dx, dz, dc in itertools.product(Y_ORDER, X_ORDER, (1, 0), (0, 1))
-    if dz + dy + dx + dc
+    sorted(
+        (d for d in itertools.product(range(NZ), range(NY), range(NX), range(NC)) if any(d)),
+        key=lambda d: (
+            -(d[0] + min(d[1], NY - d[1]) + min(d[2], NX - d[2])),
+            -min(d[1], NY - d[1]),
+            d[2],
+            d[3],
+            d[1],
+        ),
+    )
 )
 EARLY = 60
 NT = (((1,), (1,)), ((), ()))

time: 29.7 us -> 28.9 us (0.973)
  Pallas kernels: 28.9 us -> 28.1 us
    pallas_call x1, Pallas kernels: 28.9 us -> 28.1 us  [body(): pl.pallas_call(kernel, out_shape=pltpu.VMEM((512, 128), BF16), in_specs=[...]
where the time goes in v5:
time: 28.9 us; the launch traced here: 28.8 us
  Pallas kernels  28.1 us (97%)
  local copies, waits for them, and re-layouts  0.66 us (2%)
    pallas_call x1, Pallas kernels, body(): pl.pallas_call(kernel, out_shape=pltpu.VMEM((512, 128), BF16), in_specs=[...  28.1 us
    unnamed x1, local copies, waits for them, and re-layouts  0.66 us

profile of v5, /device:TPU:1, one launch (start us, length us, event | category | flops | bytes accessed | tf_op | source)
XLA Modules:
  0.0 28.8 jit_solution(16977280635541109063)
XLA Ops:
  0.0 28.1 %shard_map.82 = bf16[512,128]{1,0:T(8,128)(2,1)S(1)} custom-call(bf16[2,128,2,128]{3,2,1,0:T(2,128)(2,1)} %bitcast.3, s32[2]{0:T(128)} %mask_hbm.1, bf16[128,128]{1,0:T(8,128)(2,1)} %gl_hbm.1, bf16[128,128]{1,0:T(8,128)(2,1)} %pl_hbm.1, bf16[128,128]{1,0:T(8,128)(2,1)} %gr_hbm.1, bf16[128,128]{1,0:T(8,128)(2,1)} %pr_hbm.1, bf16[128,128]{1,0:T(8,128)(2,1)} %go_hbm.1, ...), custom_call_target="tpu_custom_call" | custom-call | tf_op jit(solution)/shard_map/pallas_call | solution.py:198
  28.1 0.7 %copy.10 = bf16[256,2,128]{2,1,0:T(2,128)(2,1)} copy(bf16[256,2,128]{2,1,0:T(2,128)(2,1)S(1)} %bitcast.2) | data formatting | bytes 262144

commit v6 on v5

--- a/solution.py
+++ b/solution.py
@@ -140,16 +140,24 @@
         for r in range(2)
     ]
     left = jnp.concatenate(lefts, axis=0).astype(BF16)
-    rights = [jnp.concatenate(halves[4 + 2 * r : 6 + 2 * r], axis=1) for r in range(2)]
-    right = jnp.concatenate(rights, axis=0).astype(BF16)
-    product = lax.dot_general(right, left, NT, preferred_element_type=F32)
-    for rj, ri in itertools.product(range(2), range(2)):
-        s4[pl.ds(2 * rj + ri, 128, stride=4), :] = product[
-            128 * rj : 128 * rj + 128, 128 * ri : 128 * ri + 128
-        ]
-    prod.reshape(512, 128)[...] = s4[...].astype(BF16)
-    for pz, py in [(0, 0), (0, 1), (0, 2), (0, 3), (1, 0), (0, 7), (1, 1), (0, 6), (0, 5), (0, 4), (1, 2), (1, 3), (1, 7), (1, 6), (1, 5), (1, 4)]:
-        for dx, dc in itertools.product(X_ORDER, (1, 0)):
+    for pz in range(NZ):
+        at = slice(64 * pz, 64 * pz + 64)
+        right = jnp.concatenate(
+            [
+                jnp.concatenate([halves[4 + 2 * r + kh][at] for kh in range(2)], axis=1)
+                for r in range(2)
+            ],
+            axis=0,
+        ).astype(BF16)
+        product = lax.dot_general(right, left, NT, preferred_element_type=F32)
+        for rj, ri in itertools.product(range(2), range(2)):
+            s4[pl.ds(256 * pz + 2 * rj + ri, 64, stride=4), :] = product[
+                64 * rj : 64 * rj + 64, 128 * ri : 128 * ri + 128
+            ]
+        prod.at[pl.ds(64 * pz, 64)].reshape(256, 128)[...] = s4[
+            pl.ds(256 * pz, 256), :
+        ].astype(BF16)
+        for py, dx, dc in itertools.product((0, 1, 2, 3, 7, 6, 5, 4), X_ORDER, (1, 0)):
             t = 64 * pz + 8 * py + xt[dx] + ct[dc]
 
             def send_prod(t=t):

time: 28.9 us -> 28.8 us (level)
  no operation moved by 1% of the time
where the time goes in v6:
time: 28.8 us; the launch traced here: 28.7 us
  Pallas kernels  28 us (97%)
  local copies, waits for them, and re-layouts  0.66 us (2%)
    pallas_call x1, Pallas kernels, body(): pl.pallas_call(kernel, out_shape=pltpu.VMEM((512, 128), BF16), in_specs=[...  28 us
    unnamed x1, local copies, waits for them, and re-layouts  0.66 us

profile of v6, /device:TPU:1, one launch (start us, length us, event | category | flops | bytes accessed | tf_op | source)
XLA Modules:
  0.0 28.7 jit_solution(10734651605249800520)
XLA Ops:
  0.0 28.0 %shard_map.82 = bf16[512,128]{1,0:T(8,128)(2,1)S(1)} custom-call(bf16[2,128,2,128]{3,2,1,0:T(2,128)(2,1)} %bitcast.3, s32[2]{0:T(128)} %mask_hbm.1, bf16[128,128]{1,0:T(8,128)(2,1)} %gl_hbm.1, bf16[128,128]{1,0:T(8,128)(2,1)} %pl_hbm.1, bf16[128,128]{1,0:T(8,128)(2,1)} %gr_hbm.1, bf16[128,128]{1,0:T(8,128)(2,1)} %pr_hbm.1, bf16[128,128]{1,0:T(8,128)(2,1)} %go_hbm.1, ...), custom_call_target="tpu_custom_call" | custom-call | tf_op jit(solution)/shard_map/pallas_call | solution.py:206
  28.0 0.7 %copy.10 = bf16[256,2,128]{2,1,0:T(2,128)(2,1)} copy(bf16[256,2,128]{2,1,0:T(2,128)(2,1)S(1)} %bitcast.2) | data formatting | bytes 262144

commit v7 on v6

--- a/solution.py
+++ b/solution.py
@@ -124,8 +124,17 @@
     for t in targets[EARLY:]:
         send(msg.at[t], fac.at[me], send_sem.at[0], fac_sem, t)
     pltpu.make_async_copy(msg.at[me], fac.at[me], fac_sem).start()
-    for t in targets:
-        send(pair_v.at[:, t], pairs.at[me], send_sem.at[1], pairs_sem, t)
+    for py, pz in itertools.product((0, 1, 2, 3, 7, 6, 5, 4), range(NZ)):
+        for dx, dc in itertools.product(X_ORDER, (1, 0)):
+            t = 64 * pz + 8 * py + xt[dx] + ct[dc]
+
+            def send_pair(t=t):
+                send(pair_v.at[:, t], pairs.at[me], send_sem.at[1], pairs_sem, t)
+
+            if dx + dc:
+                send_pair()
+            else:
+                pl.when(t != me)(send_pair)
     pltpu.make_async_copy(pair_v.at[:, me], pairs.at[me], pairs_sem).start()
     landed(my.at[pl.ds(0, 15)], mask_sem.at[3])
     mask_v[...] = jnp.sum(my[...], axis=0)

time: 28.8 us -> 28.7 us (level)
  no operation moved by 1% of the time
where the time goes in v7:
time: 28.7 us; the launch traced here: 28.6 us
  Pallas kernels  27.9 us (97%)
  local copies, waits for them, and re-layouts  0.66 us (2%)
    pallas_call x1, Pallas kernels, body(): pl.pallas_call(kernel, out_shape=pltpu.VMEM((512, 128), BF16), in_specs=[...  27.9 us
    unnamed x1, local copies, waits for them, and re-layouts  0.66 us

profile of v7, /device:TPU:1, one launch (start us, length us, event | category | flops | bytes accessed | tf_op | source)
XLA Modules:
  0.0 28.6 jit_solution(13021474311671922356)
XLA Ops:
  0.0 27.9 %shard_map.82 = bf16[512,128]{1,0:T(8,128)(2,1)S(1)} custom-call(bf16[2,128,2,128]{3,2,1,0:T(2,128)(2,1)} %bitcast.3, s32[2]{0:T(128)} %mask_hbm.1, bf16[128,128]{1,0:T(8,128)(2,1)} %gl_hbm.1, bf16[128,128]{1,0:T(8,128)(2,1)} %pl_hbm.1, bf16[128,128]{1,0:T(8,128)(2,1)} %gr_hbm.1, bf16[128,128]{1,0:T(8,128)(2,1)} %pr_hbm.1, bf16[128,128]{1,0:T(8,128)(2,1)} %go_hbm.1, ...), custom_call_target="tpu_custom_call" | custom-call | tf_op jit(solution)/shard_map/pallas_call | solution.py:215
  27.9 0.7 %copy.10 = bf16[256,2,128]{2,1,0:T(2,128)(2,1)} copy(bf16[256,2,128]{2,1,0:T(2,128)(2,1)S(1)} %bitcast.2) | data formatting | bytes 262144
